TPU v7x, 32 devices: a whole 2x2x4 slice. The times are simulated.
32 devices in a mesh: dp: 8 (over y, x, core), tp: 4 (over z).
Axes of the slice: x: 2, y: 2, z: 4, core: 2. Of those that a mesh axis runs over, the one named last changes fastest.
Arguments:
- tokens: bfloat16 [16384, 768], P(('dp', 'tp')), may hold values from -6 to 6
- w_qkv: bfloat16 [768, 2304], P('dp', 'tp'), may hold values from -0.21875 to 0.21875
- w_score: bfloat16 [768, 12], P('dp', 'tp'), may hold values from -0.21875 to 0.21875
- w_out: bfloat16 [768, 768], P('tp', 'dp'), may hold values from -0.625 to 0.625
- w_fc: bfloat16 [768, 3072], P('dp', 'tp'), may hold values from -0.21875 to 0.21875
- w_proj: bfloat16 [3072, 768], P('tp', 'dp'), may hold values from -0.15625 to 0.15625
- ln1_gain: bfloat16 [768], P('dp'), may hold values from 0.25 to 1.75
- ln2_gain: bfloat16 [768], P('dp'), may hold values from 0.25 to 1.75
- selected: int32 [256, 12, 64], P('dp', 'tp'), may hold values from 0 to 1023, as said below
- holder: int32 [8], replicated, may hold values from 0 to 1, as said below
- cotangent: bfloat16 [16384, 768], P(('dp', 'tp')), may hold values from -6 to 6
Outputs:
- output: float32 [16384, 768], P(('dp', 'tp'))
- input_grad: float32 [16384, 768], P(('dp', 'tp'))
- grad_qkv: float32 [768, 2304], P('dp', 'tp')
- grad_score: float32 [768, 12], P('dp', 'tp')
- grad_out: float32 [768, 768], P('tp', 'dp')
- grad_fc: float32 [768, 3072], P('dp', 'tp')
- grad_proj: float32 [3072, 768], P('tp', 'dp')
- grad_ln1: float32 [768], P('dp')
- grad_ln2: float32 [768], P('dp')
Inputs may be any that keep to these rules, and one draw needn't show every extreme that they name: `selected`: the 64 entries of a row are distinct positions of a prompt. `holder`: in every pair the first two groups have their prompts on different stretches.
All inputs are finite; a program needn't handle non-finite values.
Results may differ from a plain program's by a relative error of at most 0.018.
Values may be sent and summed in bfloat16 or wider, within the bound.
A program may use at most 128 MiB of HBM per device.

v0:
```python
import math

import jax
import jax.numpy as jnp
from jax import lax
from jax.sharding import PartitionSpec as P

HD = 64
WIN = 64
TOPK = 64
C = 128
NC = 8
P_SIZE = 1024
GPAIR = 2


EPS = 1e-05


def swapped(array, axis, stride):
    return lax.ppermute(array, axis, [(i, i ^ 1 << stride) for i in range(lax.axis_size(axis))])


def product(left, right):
    return jnp.dot(left, right, preferred_element_type=jnp.float32)


def times_trans(left, right):
    return lax.dot_general(
        left, right, (((1,), (1,)), ((), ())), preferred_element_type=jnp.float32
    )


def trans_times(left, right):
    return lax.dot_general(
        left, right, (((0,), (0,)), ((), ())), preferred_element_type=jnp.float32
    )


def normalize(rows):
    center = rows - jnp.mean(rows, axis=-1, keepdims=True)
    spread = jnp.mean(center * center, axis=-1, keepdims=True)
    inverse = lax.rsqrt(spread + EPS)
    return (center * inverse, inverse)


def norm_back(grad_in, normed, inverse, gain):
    inner = grad_in * gain
    return inverse * (
        inner
        - jnp.mean(inner, -1, keepdims=True)
        - normed * jnp.mean(inner * normed, -1, keepdims=True)
    )


def per_device(
    tokens, w_qkv, w_score, w_out, w_fc, w_proj, ln1_gain, ln2_gain, selected, holder, cotangent
):
    whole = (
        lax.all_gather(w_qkv, "dp", axis=0, tiled=True),
        lax.all_gather(w_score, "dp", axis=0, tiled=True),
        lax.all_gather(w_out, "dp", axis=1, tiled=True),
        lax.all_gather(w_fc, "dp", axis=0, tiled=True),
        lax.all_gather(w_proj, "dp", axis=1, tiled=True),
        lax.all_gather(ln1_gain, "dp", axis=0, tiled=True),
        lax.all_gather(ln2_gain, "dp", axis=0, tiled=True),
    )
    whole_qkv, whole_score, whole_out, whole_fc, whole_proj, gain_one, gain_two = whole
    parts = lax.axis_size("tp")
    local_rows = tokens.shape[0]
    rows = local_rows * parts
    heads = whole_score.shape[1]
    blocks = rows // WIN
    scale = 1.0 / math.sqrt(HD)
    side = lax.axis_index("dp") % 2
    pair_index = lax.axis_index("dp") // 2
    holds = lax.dynamic_slice_in_dim(holder, pair_index * GPAIR, GPAIR, 0)
    prompt_flag = (holds == side).astype(jnp.int32)
    stream = tokens.astype(jnp.float32)
    normed_one, inverse_one = normalize(stream)
    first_low = (normed_one * gain_one.astype(jnp.float32)).astype(jnp.bfloat16)
    first_full = lax.all_gather(first_low, "tp", axis=0, tiled=True)
    mixed = product(first_full, whole_qkv).astype(jnp.bfloat16).reshape(rows, heads, 3, HD)
    queries = mixed[:, :, 0]
    keys_near = mixed[:, :, 1]
    values_near = mixed[:, :, 2]
    raw_gate = product(first_full, whole_score)
    gate_low = jax.nn.log_sigmoid(raw_gate).astype(jnp.bfloat16)
    far_keys, far_values, far_gate = swapped((keys_near, values_near, gate_low), "dp", 0)
    position = jnp.arange(rows)
    unit = position // P_SIZE
    unit_prompt = (
        jnp.sum(
            jnp.where(unit[:, None] == jnp.arange(GPAIR)[None, :], prompt_flag[None, :], 0), axis=1
        )
        > 0
    )
    segment = unit * (NC + 1) + jnp.where(unit_prompt, NC, position % P_SIZE // C)
    query_pos = position.reshape(blocks, WIN)
    key_pos = query_pos[:, :1] - WIN + jnp.arange(2 * WIN)[None, :]
    distance = query_pos[:, :, None] - key_pos[:, None, :]
    query_seg = segment.reshape(blocks, WIN)
    earlier_seg = jnp.concatenate([jnp.full((WIN,), -1, jnp.int32), segment[:-WIN]]).reshape(
        blocks, WIN
    )
    key_seg = jnp.concatenate([earlier_seg, query_seg], 1)
    near_ok = (distance >= 0) & (distance < WIN) & (key_seg[:, None, :] == query_seg[:, :, None])
    block_unit = jnp.arange(blocks) * WIN // P_SIZE
    far_ok = jnp.logical_not(unit_prompt.reshape(blocks, WIN)[:, 0])
    picked = (
        (block_unit[:, None, None] * P_SIZE + selected)
        .transpose(1, 0, 2)
        .reshape(heads, blocks * TOPK)
    )

    def pick(table):
        gathered = jnp.take_along_axis(table.transpose(1, 0, 2), picked[:, :, None], axis=1)
        return gathered.reshape(heads, blocks, TOPK, HD)

    sel_keys = pick(far_keys)
    sel_values = pick(far_values)
    sel_gate = (
        jnp.take_along_axis(far_gate.T, picked, axis=1)
        .reshape(heads, blocks, TOPK)
        .astype(jnp.float32)
    )

    def framed(table):
        earlier = jnp.concatenate(
            [jnp.zeros((WIN, heads, HD), table.dtype), table[:-WIN]], 0
        ).reshape(blocks, WIN, heads, HD)
        return jnp.concatenate([earlier, table.reshape(blocks, WIN, heads, HD)], 1)

    block_keys = framed(keys_near)
    block_values = framed(values_near)
    block_queries = queries.reshape(blocks, WIN, heads, HD)
    near = (
        jnp.einsum("bqhd,bkhd->bhqk", block_queries, block_keys, preferred_element_type=jnp.float32)
        * scale
    )
    far = (
        jnp.einsum("bqhd,hbtd->bhqt", block_queries, sel_keys, preferred_element_type=jnp.float32)
        * scale
    )
    far = far + sel_gate.transpose(1, 0, 2)[:, :, None, :]
    logits = jnp.concatenate([near, far], -1)
    valid = jnp.concatenate(
        [
            jnp.broadcast_to(near_ok[:, None], near.shape),
            jnp.broadcast_to(far_ok[:, None, None, None], far.shape),
        ],
        -1,
    )
    top = jnp.max(jnp.where(valid, logits, -1e30), -1, keepdims=True)
    raised = jnp.exp(jnp.where(valid, logits - top, -1e30))
    shares = raised / jnp.sum(raised, -1, keepdims=True)
    shares_low = shares.astype(jnp.bfloat16)
    attended = jnp.einsum(
        "bhqk,bkhd->bqhd",
        shares_low[..., : 2 * WIN],
        block_values,
        preferred_element_type=jnp.float32,
    )
    attended = attended + jnp.einsum(
        "bhqt,hbtd->bqhd",
        shares_low[..., 2 * WIN :],
        sel_values,
        preferred_element_type=jnp.float32,
    )
    attended = attended.reshape(rows, heads * HD).astype(jnp.bfloat16)
    branch = lax.psum_scatter(
        product(attended, whole_out).astype(jnp.bfloat16), "tp", scatter_dimension=0, tiled=True
    ).astype(jnp.float32)
    resid = stream + branch
    normed_two, inverse_two = normalize(resid)
    second_low = (normed_two * gain_two.astype(jnp.float32)).astype(jnp.bfloat16)
    second_full = lax.all_gather(second_low, "tp", axis=0, tiled=True)
    pre_act = product(second_full, whole_fc)
    hidden = jax.nn.gelu(pre_act).astype(jnp.bfloat16)
    output = resid + lax.psum_scatter(
        product(hidden, whole_proj).astype(jnp.bfloat16), "tp", scatter_dimension=0, tiled=True
    ).astype(jnp.float32)
    upstream_full = lax.all_gather(cotangent, "tp", axis=0, tiled=True)
    grad_proj = trans_times(hidden, upstream_full)
    grad_hidden = times_trans(upstream_full, whole_proj)
    grad_pre = jax.vjp(jax.nn.gelu, pre_act)[1](grad_hidden)[0].astype(jnp.bfloat16)
    grad_fc = trans_times(second_full, grad_pre)
    grad_second = lax.psum_scatter(
        times_trans(grad_pre, whole_fc), "tp", scatter_dimension=0, tiled=True
    )
    ln2_part = jnp.sum(grad_second * normed_two, 0)
    grad_resid = cotangent.astype(jnp.float32) + norm_back(
        grad_second, normed_two, inverse_two, gain_two.astype(jnp.float32)
    )
    branch_full = lax.all_gather(grad_resid.astype(jnp.bfloat16), "tp", axis=0, tiled=True)
    grad_out = trans_times(attended, branch_full)
    grad_att = (
        times_trans(branch_full, whole_out).astype(jnp.bfloat16).reshape(blocks, WIN, heads, HD)
    )
    grad_near = jnp.einsum(
        "bqhd,bkhd->bhqk", grad_att, block_values, preferred_element_type=jnp.float32
    )
    grad_far = jnp.einsum(
        "bqhd,hbtd->bhqt", grad_att, sel_values, preferred_element_type=jnp.float32
    )
    grad_shares = jnp.concatenate([grad_near, grad_far], -1)
    grad_logits = (
        shares * (grad_shares - jnp.sum(shares * grad_shares, -1, keepdims=True))
    ).astype(jnp.bfloat16)
    logit_near = grad_logits[..., : 2 * WIN]
    logit_far = grad_logits[..., 2 * WIN :]
    grad_queries = jnp.einsum(
        "bhqk,bkhd->bqhd", logit_near, block_keys, preferred_element_type=jnp.float32
    )
    grad_queries = grad_queries + jnp.einsum(
        "bhqt,hbtd->bqhd", logit_far, sel_keys, preferred_element_type=jnp.float32
    )
    grad_queries = (grad_queries * scale).reshape(rows, heads, HD).astype(jnp.bfloat16)
    grad_block_keys = (
        jnp.einsum("bhqk,bqhd->bkhd", logit_near, block_queries, preferred_element_type=jnp.float32)
        * scale
    )
    grad_block_values = jnp.einsum(
        "bhqk,bqhd->bkhd", shares_low[..., : 2 * WIN], grad_att, preferred_element_type=jnp.float32
    )

    def unframe(grads):
        earlier = grads[:, :WIN].reshape(rows, heads, HD)
        own_part = grads[:, WIN:].reshape(rows, heads, HD)
        return own_part + jnp.concatenate(
            [earlier[WIN:], jnp.zeros((WIN, heads, HD), jnp.float32)], 0
        )

    near_dkeys = unframe(grad_block_keys)
    near_dvalues = unframe(grad_block_values)
    sel_dkeys = (
        jnp.einsum("bhqt,bqhd->hbtd", logit_far, block_queries, preferred_element_type=jnp.float32)
        * scale
    )
    sel_dvalues = jnp.einsum(
        "bhqt,bqhd->hbtd", shares_low[..., 2 * WIN :], grad_att, preferred_element_type=jnp.float32
    )
    sel_dgate = jnp.sum(logit_far.astype(jnp.float32), axis=2).transpose(1, 0, 2)
    flat_index = (jnp.arange(heads)[:, None] * rows + picked).reshape(-1)

    def place(entries, width):
        spread_out = (
            jnp.zeros((heads * rows, width), jnp.float32)
            .at[flat_index]
            .add(entries.reshape(heads * blocks * TOPK, width))
        )
        return spread_out.reshape(heads, rows, width).transpose(1, 0, 2)

    far_dkeys = place(sel_dkeys, HD)
    far_dvalues = place(sel_dvalues, HD)
    far_dgate = place(sel_dgate[..., None], 1)[:, :, 0]
    back_keys, back_values, back_gate = (
        swapped(far_dkeys.astype(jnp.bfloat16), "dp", 0).astype(far_dkeys.dtype),
        swapped(far_dvalues.astype(jnp.bfloat16), "dp", 0).astype(far_dvalues.dtype),
        swapped(far_dgate.astype(jnp.bfloat16), "dp", 0).astype(far_dgate.dtype),
    )
    grad_keys = (near_dkeys + back_keys).astype(jnp.bfloat16)
    grad_values = (near_dvalues + back_values).astype(jnp.bfloat16)
    grad_raw = (back_gate * jax.nn.sigmoid(-raw_gate)).astype(jnp.bfloat16)
    grad_mixed = jnp.stack([grad_queries, grad_keys, grad_values], axis=2).reshape(
        rows, 3 * heads * HD
    )
    grad_qkv = trans_times(first_full, grad_mixed)
    grad_score = trans_times(first_full, grad_raw)
    grad_first = lax.psum_scatter(
        (times_trans(grad_mixed, whole_qkv) + times_trans(grad_raw, whole_score)).astype(
            jnp.bfloat16
        ),
        "tp",
        scatter_dimension=0,
        tiled=True,
    ).astype(jnp.float32)
    ln1_part = jnp.sum(grad_first * normed_one, 0)
    input_grad = grad_resid + norm_back(
        grad_first, normed_one, inverse_one, gain_one.astype(jnp.float32)
    )
    ln1_total, ln2_total = lax.psum((ln1_part, ln2_part), "tp")
    reduced = (
        lax.psum_scatter(grad_qkv, "dp", scatter_dimension=0, tiled=True),
        lax.psum_scatter(grad_score, "dp", scatter_dimension=0, tiled=True),
        lax.psum_scatter(grad_out, "dp", scatter_dimension=1, tiled=True),
        lax.psum_scatter(grad_fc, "dp", scatter_dimension=0, tiled=True),
        lax.psum_scatter(grad_proj, "dp", scatter_dimension=1, tiled=True),
        lax.psum_scatter(ln1_total, "dp", scatter_dimension=0, tiled=True),
        lax.psum_scatter(ln2_total, "dp", scatter_dimension=0, tiled=True),
    )
    return (
        output,
        input_grad,
        reduced[0],
        reduced[1],
        reduced[2],
        reduced[3],
        reduced[4],
        reduced[5],
        reduced[6],
    )


def solution(mesh):
    in_specs = (
        P(("dp", "tp"), None),
        P("dp", "tp"),
        P("dp", "tp"),
        P("tp", "dp"),
        P("dp", "tp"),
        P("tp", "dp"),
        P("dp"),
        P("dp"),
        P("dp", "tp", None),
        P(),
        P(("dp", "tp"), None),
    )
    out_specs = (
        P(("dp", "tp"), None),
        P(("dp", "tp"), None),
        P("dp", "tp"),
        P("dp", "tp"),
        P("tp", "dp"),
        P("dp", "tp"),
        P("tp", "dp"),
        P("dp"),
        P("dp"),
    )
    return jax.shard_map(
        per_device, mesh=mesh, in_specs=in_specs, out_specs=out_specs, check_vma=False
    )
```

profile of v0, /device:TPU:0, one launch (start us, length us, event | category | flops | bytes accessed | tf_op | source)
XLA Modules:
  0.0 1300.0 jit_solution(1578480374674993637)
XLA Ops:
  14.7 15.7 %all-reduce.11 = (bf16[768]{0:T(1024)(128)(2,1)}, bf16[768]{0:T(1024)(128)(2,1)S(1)}) all-reduce(bf16[768]{0:T(1024)(128)(2,1)S(1)} %dynamic-update-slice.1, bf16[768]{0:T(1024)(128)(2,1)S(1)} %dynamic-update-slice), channel_id=1, replica_groups=mesh['dp'=8,'tp'=4] {'dp'}, use_global_device_ids=true, to_apply=%add.6 | all-reduce | flops 1536 | bytes 6144
  64.8 30.9 %all-gather.8.cloned.1.call-done = bf16[2048,768]{1,0:T(8,128)(2,1)} async-done(((bf16[512,768]{1,0:T(8,128)(2,1)}), bf16[2048,768]{1,0:T(8,128)(2,1)}) %all-gather.8.cloned.1.call-update) | async-done | bytes 3145744 | tf_op jit(solution)/shard_map/all_gather | solution.py:82
  130.2 52.4 %gather_fusion = bf16[6144]{0:T(1024)(128)(2,1)S(1)} fusion(bf16[3,2048]{1,0:T(4,128)(2,1)S(1)} %bitcast.159, s32[6144]{0:T(1024)S(1)} %reshape.426), kind=kCustom, calls=%fused_computation.2 | custom fusion | bytes 73728 | tf_op jit(solution)/shard_map/jit(take_along_axis)/gather | solution.py:123
  185.3 60.6 %gather_fusion.2 = bf16[6144,64]{1,0:T(8,128)(2,1)} fusion(bf16[3,2048,64]{2,1,0:T(8,128)(2,1)S(1)} %bitcast.161, s32[6144]{0:T(1024)S(1)} %reshape.426), kind=kCustom, calls=%fused_computation.1.clone | custom fusion | bytes 1622016 | tf_op jit(solution)/shard_map/jit(take_along_axis)/gather | solution.py:117
  250.1 60.6 %gather_fusion.1 = bf16[6144,64]{1,0:T(8,128)(2,1)} fusion(bf16[3,2048,64]{2,1,0:T(8,128)(2,1)S(1)} %bitcast.160, s32[6144]{0:T(1024)S(1)} %reshape.426), kind=kCustom, calls=%fused_computation.clone | custom fusion | bytes 1622016 | tf_op jit(solution)/shard_map/jit(take_along_axis)/gather | solution.py:117
  325.8 17.5 %fusion.109 = (f32[32,3,64]{2,1,0:T(4,128)S(1)}, f32[32,3,64,192]{3,2,1,0:T(8,128)S(1)}) fusion(f32[32,3,64,64]{3,2,1,0:T(8,128)S(1)} %multiply_add_fusion, f32[32,3,64,128]{3,2,1,0:T(8,128)S(1)} %copy-done.25, pred[32,3,64,64]{3,2,1,0:T(8,128)(4,1)S(1)} %broadcast_in_dim.44, pred[32,3,64,128]{3,2,1,0:T(8,128)(4,1)S(1)} %broadcast_in_dim.43), kind=kOutput, calls=%fused_computation.221 | output fusion | flops 9437375 | bytes 10641408 | tf_op jit(solution)/shard_map/sub | solution.py:155
  360.5 74.5 %reduce-scatter.14.cloned.1.call-done = bf16[512,768]{1,0:T(8,128)(2,1)} async-done(((bf16[2048,768]{1,0:T(8,128)(2,1)}), bf16[512,768]{1,0:T(8,128)(2,1)}) %reduce-scatter.14.cloned.1.call-update) | async-done | bytes 786448 | tf_op jit(solution)/shard_map/reduce_scatter | solution.py:171
  439.3 29.1 %all-gather.16.cloned.1.call-done = bf16[2048,768]{1,0:T(8,128)(2,1)} async-done(((bf16[512,768]{1,0:T(8,128)(2,1)}), bf16[2048,768]{1,0:T(8,128)(2,1)}) %all-gather.16.cloned.1.call-update) | async-done | bytes 3145744 | tf_op jit(solution)/shard_map/all_gather | solution.py:183
  475.9 17.9 %all-gather.12.cloned.1.call-done = bf16[768,768]{1,0:T(8,128)(2,1)} async-done(((bf16[96,768]{1,0:T(8,128)(2,1)}), bf16[768,768]{1,0:T(8,128)(2,1)}) %all-gather.12.cloned.1.call-update) | async-done | bytes 1179664 | tf_op jit(solution)/shard_map/all_gather | solution.py:63
  493.8 65.5 %all-gather.10.cloned.1.call-done = bf16[2048,768]{1,0:T(8,128)(2,1)} async-done(((bf16[512,768]{1,0:T(8,128)(2,1)}), bf16[2048,768]{1,0:T(8,128)(2,1)}) %all-gather.10.cloned.1.call-update) | async-done | bytes 3145744 | tf_op jit(solution)/shard_map/all_gather | solution.py:177
  559.3 11.0 fusion.8
  585.5 100.8 %reduce-scatter.18.cloned.1.call-done = f32[512,768]{1,0:T(8,128)} async-done(((f32[2048,768]{1,0:T(8,128)}), f32[512,768]{1,0:T(8,128)}) %reduce-scatter.18.cloned.1.call-update) | async-done | bytes 1572880 | tf_op jit(solution)/shard_map/reduce_scatter | solution.py:188
  688.4 60.8 %reduce-scatter.16.cloned.1.call-done = bf16[512,768]{1,0:T(8,128)(2,1)} async-done(((bf16[2048,768]{1,0:T(8,128)(2,1)}), bf16[512,768]{1,0:T(8,128)(2,1)}) %reduce-scatter.16.cloned.1.call-update) | async-done | bytes 786448 | tf_op jit(solution)/shard_map/reduce_scatter | solution.py:180
  754.1 63.2 %all-gather.18.cloned.1.call-done = bf16[2048,768]{1,0:T(8,128)(2,1)} async-done(((bf16[512,768]{1,0:T(8,128)(2,1)}), bf16[2048,768]{1,0:T(8,128)(2,1)}) %all-gather.18.cloned.1.call-update) | async-done | bytes 3145744 | tf_op jit(solution)/shard_map/all_gather | solution.py:195
  828.6 36.7 %multiply_convert_fusion = bf16[32,3,64,192]{3,2,1,0:T(8,128)(2,1)S(1)} fusion(f32[32,3,64,64]{3,2,1,0:T(8,128)S(1)} %fusion.48, f32[32,3,64,128]{3,2,1,0:T(8,128)S(1)} %fusion.50, f32[32,3,64,192]{3,2,1,0:T(8,128)} %copy-done.19, f32[32,3,64]{2,1,0:T(4,128)S(1)} %get-tuple-element.38), kind=kOutput, calls=%fused_computation.20 | output fusion | flops 9443519 | bytes 11821056 | tf_op jit(solution)/shard_map/sub | solution.py:208
  877.5 43.1 %scatter_custom_fusion.2 = f32[6144]{0:T(1024)S(1)} fusion(s32[6144]{0:T(1024)S(1)} %bitcast.175, f32[6144]{0:T(1024)S(1)} %reshape.406, f32[]{:T(128)} %constant.158.clone.1), kind=kCustom, calls=%fused_computation.169 | custom fusion | flops 6144 | bytes 24580 | tf_op jit(solution)/shard_map/scatter-add | solution.py:250
  920.7 35.4 %scatter_custom_fusion = f32[6144,64]{1,0:T(8,128)} fusion(s32[6144]{0:T(1024)S(1)} %bitcast.176, f32[6144,64]{1,0:T(8,128)} %bitcast.166, f32[]{:T(128)} %constant.158.clone.1), kind=kCustom, calls=%fused_computation.74 | custom fusion | flops 393216 | bytes 1573376 | tf_op jit(solution)/shard_map/scatter-add | solution.py:250
  963.9 35.3 %scatter_custom_fusion.1 = f32[6144,64]{1,0:T(8,128)} fusion(s32[6144]{0:T(1024)S(1)} %bitcast.177, f32[6144,64]{1,0:T(8,128)} %bitcast.167, f32[]{:T(128)} %constant.158.clone.1), kind=kCustom, calls=%fused_computation.72 | custom fusion | flops 393216 | bytes 1573376 | tf_op jit(solution)/shard_map/scatter-add | solution.py:250
  1096.3 59.3 %reduce-scatter.20.cloned.1.call-done = bf16[512,768]{1,0:T(8,128)(2,1)} async-done(((bf16[2048,768]{1,0:T(8,128)(2,1)}), bf16[512,768]{1,0:T(8,128)(2,1)}) %reduce-scatter.20.cloned.1.call-update) | async-done | bytes 786448 | tf_op jit(solution)/shard_map/reduce_scatter | solution.py:270
  1157.6 13.5 %all-reduce.9 = (f32[768]{0:T(1024)S(1)}, f32[768]{0:T(1024)S(1)}) all-reduce(f32[768]{0:T(1024)S(1)} %get-tuple-element.13, f32[768]{0:T(1024)S(1)} %get-tuple-element.10), channel_id=11, replica_groups=mesh['dp'=8,'tp'=4] {'dp'}, use_global_device_ids=true, to_apply=%region_27.29.clone | all-reduce | flops 1536 | bytes 12288
  1171.2 11.4 all-reduce.10
  1185.5 16.2 %reduce-scatter.24.cloned.1.call-done = f32[96,768]{1,0:T(8,128)} async-done(((f32[768,768]{1,0:T(8,128)}), f32[96,768]{1,0:T(8,128)}) %reduce-scatter.24.cloned.1.call-update) | async-done | bytes 294928 | tf_op jit(solution)/shard_map/reduce_scatter | solution.py:287
  1201.7 46.7 %reduce-scatter.26.cloned.1.call-done = f32[768,96]{0,1:T(8,128)} async-done(((f32[768,768]{0,1:T(8,128)}), f32[768,96]{0,1:T(8,128)}) %reduce-scatter.26.cloned.1.call-update) | async-done | bytes 294928 | tf_op jit(solution)/shard_map/reduce_scatter | solution.py:288
  1248.4 44.0 %reduce-scatter.22.cloned.1.call-done = f32[96,576]{1,0:T(8,128)} async-done(((f32[768,576]{1,0:T(8,128)}), f32[96,576]{1,0:T(8,128)}) %reduce-scatter.22.cloned.1.call-update) | async-done | bytes 221200 | tf_op jit(solution)/shard_map/reduce_scatter | solution.py:284
  (290 shorter events, 279.9 us)
Async XLA Ops:
  8.1 87.7 %all-gather.8.cloned.1.call-start = ((), (), s32[]{:S(2)}) async-start(), calls=%async_computation.9 | async-start | bytes 3932160 | tf_op jit(solution)/shard_map/all_gather | solution.py:82
  32.7 402.2 %reduce-scatter.14.cloned.1.call-start = ((), (), s32[]{:S(2)}) async-start(), calls=%async_computation.10 | async-start | bytes 3932160 | tf_op jit(solution)/shard_map/reduce_scatter | solution.py:171
  102.9 80.6 %collective-permute-start.2 = (bf16[2048,3,64]{0,2,1:T(8,128)(2,1)}, bf16[2048,3,64]{0,2,1:T(8,128)(2,1)}, u32[]{:S(2)}, u32[]{:S(2)}) collective-permute-start(bf16[2048,3,64]{0,2,1:T(8,128)(2,1)} %get-tuple-element.24), channel_id=1, source_target_pairs={{0,4},{4,0},{8,12},{12,8},{16,20},{20,16},{24,28},{28,24},{1,5},{5... | collective-permute-start | bytes 2359304 | tf_op jit(solution)/shard_map/ppermute | solution.py:21
  102.9 145.4 %collective-permute-start = (bf16[2048,3,64]{0,2,1:T(8,128)(2,1)}, bf16[2048,3,64]{0,2,1:T(8,128)(2,1)}, u32[]{:S(2)}, u32[]{:S(2)}) collective-permute-start(bf16[2048,3,64]{0,2,1:T(8,128)(2,1)} %get-tuple-element.25), channel_id=1, source_target_pairs={{0,4},{4,0},{8,12},{12,8},{16,20},{20,16},{24,28},{28,24},{1,5},{5... | collective-permute-start | bytes 2359304 | tf_op jit(solution)/shard_map/ppermute | solution.py:21
  105.0 25.2 %collective-permute-start.1 = (bf16[2048,3]{0,1:T(4,128)(2,1)S(1)}, bf16[2048,3]{0,1:T(4,128)(2,1)S(1)}, u32[]{:S(2)}, u32[]{:S(2)}) collective-permute-start(bf16[2048,3]{0,1:T(4,128)(2,1)S(1)} %get-tuple-element.36), channel_id=1, source_target_pairs={{0,4},{4,0},{8,12},{12,8},{16,20},{20,16},{24,28},{28,24},{1,5},{5... | collective-permute-start | bytes 36872 | tf_op jit(solution)/shard_map/ppermute | solution.py:21
  358.6 76.3 %copy-start = (bf16[512,768]{1,0:T(8,128)(2,1)S(1)}, bf16[512,768]{1,0:T(8,128)(2,1)}, u32[]{:S(2)}) copy-start(bf16[512,768]{1,0:T(8,128)(2,1)} %param.13) | copy-start | bytes 2359300
  358.7 80.7 %all-gather.14.cloned.1.call-start = ((), (), s32[]{:S(2)}) async-start(), calls=%async_computation.13 | async-start | bytes 1327104 | tf_op jit(solution)/shard_map/all_gather | solution.py:64
  359.2 109.2 %all-gather.16.cloned.1.call-start = ((), (), s32[]{:S(2)}) async-start(), calls=%async_computation.15 | async-start | bytes 3932160 | tf_op jit(solution)/shard_map/all_gather | solution.py:183
  359.8 134.0 %all-gather.12.cloned.1.call-start = ((), (), s32[]{:S(2)}) async-start(), calls=%async_computation.12 | async-start | bytes 1327104 | tf_op jit(solution)/shard_map/all_gather | solution.py:63
  360.4 198.9 %all-gather.10.cloned.1.call-start = ((), (), s32[]{:S(2)}) async-start(), calls=%async_computation.11 | async-start | bytes 3932160 | tf_op jit(solution)/shard_map/all_gather | solution.py:177
  439.3 247.0 %reduce-scatter.18.cloned.1.call-start = ((), (), s32[]{:S(2)}) async-start(), calls=%async_computation.16 | async-start | bytes 7864320 | tf_op jit(solution)/shard_map/reduce_scatter | solution.py:188
  576.7 172.5 %reduce-scatter.16.cloned.1.call-start = ((), (), s32[]{:S(2)}) async-start(), calls=%async_computation.14 | async-start | bytes 3932160 | tf_op jit(solution)/shard_map/reduce_scatter | solution.py:180
  585.4 231.9 %all-gather.18.cloned.1.call-start = ((), (), s32[]{:S(2)}) async-start(), calls=%async_computation.17 | async-start | bytes 3932160 | tf_op jit(solution)/shard_map/all_gather | solution.py:195
  753.8 339.4 %reduce-scatter.28.cloned.1.call-start = ((), (), s32[]{:S(2)}) async-start(), calls=%async_computation.22 | async-start | bytes 442368
  920.6 81.7 %collective-permute-start.5 = (bf16[2048,3]{0,1:T(4,128)(2,1)S(1)}, bf16[2048,3]{0,1:T(4,128)(2,1)S(1)}, u32[]{:S(2)}, u32[]{:S(2)}) collective-permute-start(bf16[2048,3]{0,1:T(4,128)(2,1)S(1)} %bitcast.178), channel_id=1, source_target_pairs={{0,4},{4,0},{8,12},{12,8},{16,20},{20,16},{24,28},{28,24},{1,5},{5... | collective-permute-start | bytes 36872 | tf_op jit(solution)/shard_map/ppermute | solution.py:21
  959.3 100.6 %collective-permute-start.3 = (bf16[2048,3,64]{0,2,1:T(8,128)(2,1)}, bf16[2048,3,64]{0,2,1:T(8,128)(2,1)}, u32[]{:S(2)}, u32[]{:S(2)}) collective-permute-start(bf16[2048,3,64]{0,2,1:T(8,128)(2,1)} %bitcast.158), channel_id=1, source_target_pairs={{0,4},{4,0},{8,12},{12,8},{16,20},{20,16},{24,28},{28,24},{1,5},{5... | collective-permute-start | bytes 2359304 | tf_op jit(solution)/shard_map/ppermute | solution.py:21
  1002.3 59.7 %collective-permute-start.4 = (bf16[2048,3,64]{0,2,1:T(8,128)(2,1)}, bf16[2048,3,64]{0,2,1:T(8,128)(2,1)}, u32[]{:S(2)}, u32[]{:S(2)}) collective-permute-start(bf16[2048,3,64]{0,2,1:T(8,128)(2,1)} %bitcast.156), channel_id=1, source_target_pairs={{0,4},{4,0},{8,12},{12,8},{16,20},{20,16},{24,28},{28,24},{1,5},{5... | collective-permute-start | bytes 2359304 | tf_op jit(solution)/shard_map/ppermute | solution.py:21
  1006.0 88.7 %reduce-scatter.30.cloned.1.call-start = ((), (), s32[]{:S(2)}) async-start(), calls=%async_computation.23 | async-start | bytes 884736
  1059.4 96.2 %reduce-scatter.20.cloned.1.call-start = ((), (), s32[]{:S(2)}) async-start(), calls=%async_computation.18 | async-start | bytes 3932160 | tf_op jit(solution)/shard_map/reduce_scatter | solution.py:270
  1070.9 130.8 %reduce-scatter.24.cloned.1.call-start = ((), (), s32[]{:S(2)}) async-start(), calls=%async_computation.20 | async-start | bytes 2654208 | tf_op jit(solution)/shard_map/reduce_scatter | solution.py:287
  1078.0 170.4 %reduce-scatter.26.cloned.1.call-start = ((), (), s32[]{:S(2)}) async-start(), calls=%async_computation.21 | async-start | bytes 2654208 | tf_op jit(solution)/shard_map/reduce_scatter | solution.py:288
  1086.3 69.3 %copy-start.33 = (f32[768]{0:T(1024)S(1)}, f32[768]{0:T(1024)}, u32[]{:S(2)}) copy-start(f32[768]{0:T(1024)} %copy-done.32) | copy-start | bytes 9220
  1086.3 206.1 %reduce-scatter.22.cloned.1.call-start = ((), (), s32[]{:S(2)}) async-start(), calls=%async_computation.19 | async-start | bytes 2211840 | tf_op jit(solution)/shard_map/reduce_scatter | solution.py:284
  1092.4 90.2 %copy-start.20 = (f32[512,768]{1,0:T(8,128)S(1)}, f32[512,768]{1,0:T(8,128)}, u32[]{:S(2)}) copy-start(f32[512,768]{1,0:T(8,128)} %get-tuple-element.23) | copy-start | bytes 4718596
  (46 other events, 755.5 us)
Sparse Core Ops, SparseCore 0:
  32.8 62.8 all-gather.7
  358.8 76.1 reduce-scatter.13
  576.8 109.3 reduce-scatter.17
  688.4 60.7 reduce-scatter.15
Sparse Core Ops, SparseCore 1:
  361.0 22.6 all-gather.13
  385.2 83.2 all-gather.15
  470.2 23.5 all-gather.11
  496.0 63.3 all-gather.9
  753.9 63.3 all-gather.17
  1006.1 32.6 reduce-scatter.27
  1059.5 33.6 reduce-scatter.29
  1095.3 60.2 reduce-scatter.19
  1159.4 42.2 reduce-scatter.23
  1206.0 42.3 reduce-scatter.25
  1252.2 40.1 reduce-scatter.21
where the time goes:
time: 1310 us; the launch traced here: 1300 us
  waiting for transfers between devices  611 us (47%)
  local copies, waits for them, and re-layouts  293 us (22%)
  other arithmetic  199 us (15%)
  matrix products  107 us (8%)
  blocking collectives  69.3 us (5%)
  between operations  18.1 us (1%)
    gather x5, local copies, waits for them, and re-layouts, pick(): jnp.take_along_axis(table.transpose(1, 0, 2), picked[:, :, None], axis=1)  125 us
    scatter-add x3, other arithmetic, place(): spread_out = jnp.zeros((heads * rows, width), jnp.float32).at[flat_index]...  114 us
    reduce_scatter x1, waiting for transfers between devices, per_device(): lax.psum_scatter(times_trans(grad_pre, whole_fc), 'tp', scatter_dimension...  101 us
    reduce_scatter x1, waiting for transfers between devices, per_device(): lax.psum_scatter(product(attended, whole_out).astype(jnp.bfloat16), 'tp',...  74.5 us
    all_gather x1, waiting for transfers between devices, per_device(): second_full = lax.all_gather(second_low, 'tp', axis=0, tiled=True)  65.5 us
    all_gather x1, waiting for transfers between devices, per_device(): lax.all_gather(grad_resid.astype(jnp.bfloat16), 'tp', axis=0, tiled=True)  63.2 us
    reduce_scatter x1, waiting for transfers between devices, per_device(): lax.psum_scatter(product(hidden, whole_proj).astype(jnp.bfloat16), 'tp',...  60.8 us
    reduce_scatter x1, waiting for transfers between devices, per_device(): lax.psum_scatter((times_trans(grad_mixed, whole_qkv) + times_trans(grad_r...  59.3 us
  transfers between devices with their start and end apart: 21, of which 12 were waited for; matrix products, arithmetic and copies ran while one was open for 27% of the time, Pallas kernels for 0%

commit v1 on v0

--- a/solution.py
+++ b/solution.py
@@ -1,8 +1,11 @@
+import functools
 import math
 
 import jax
 import jax.numpy as jnp
 from jax import lax
+from jax.experimental import pallas as pl
+from jax.experimental.pallas import tpu as pltpu
 from jax.sharding import PartitionSpec as P
 
 HD = 64
@@ -53,19 +56,153 @@
     )
 
 
+MESH = pl.DeviceIdType.MESH
+COLS = (640, 256, 768, 768)
+OFF = (0, 640, 896, 1664)
+WIDE = 2432
+TP = 4
+
+class Place:
+    def __init__(self, inner):
+        self.inner = inner
+        self.dp = lax.axis_index("dp")
+        self.z = lax.axis_index("tp")
+        self.k = self.dp // inner
+        self.cb = self.k % 2
+        self.yx = self.k // 2
+        self.step = inner
+        self.core = (self.flip(1), self.z)
+        self.xn = (self.flip(2), self.z)
+        self.yn = (self.flip(4), self.z)
+    def flip(self, bit):
+        d = self.k // bit % 2
+        return self.dp + (1 - 2 * d) * bit * self.inner
+    def zdev(self, s):
+        return (self.dp, (self.z + s) % TP)
+
+def barrier(devs):
+    b = pltpu.get_barrier_semaphore()
+    for d in devs:
+        pl.semaphore_signal(b, inc=1, device_id=d, device_id_type=MESH)
+    pl.semaphore_wait(b, len(devs))
+
+class Gather:
+    def __init__(self, at, own, bufs, sems):
+        self.at, self.own, self.bufs = at, own, bufs
+        self.zs, self.zr, self.ps, self.pr = sems
+    def put(self, src, dst, ssem, rsem, dev):
+        return pltpu.make_async_remote_copy(src_ref=src, dst_ref=dst, send_sem=ssem, recv_sem=rsem, device_id=dev, device_id_type=MESH)
+    def slot(self, s):
+        return (self.at.z - s + TP) % TP
+    def c_z(self, p, s):
+        a = self.at
+        return self.put(self.own[p], self.bufs[p].at[a.z, a.yx, a.cb], self.zs.at[p, s-1], self.zr.at[p, s-1], a.zdev(s))
+    def c_xy(self, p, s, j):
+        a = self.at
+        r = self.bufs[p].at[self.slot(s), a.yx, a.cb]
+        return self.put(r, r, self.ps.at[p, s, j], self.pr.at[p, s, j], (a.xn, a.yn)[j])
+    def c_half(self, p, s, j):
+        a = self.at
+        h = self.bufs[p].shape[3] // 2
+        other = a.yx + (1 - 2 * (a.yx % 2)) if j == 0 else a.yx + (1 - 2 * (a.yx // 2)) * 2
+        r = self.bufs[p].at[self.slot(s), other, a.cb, pl.ds(j * h, h)]
+        return self.put(r, r, self.ps.at[p, s, 2 + j], self.pr.at[p, s, 2 + j], (a.yn, a.xn)[j])
+    def c_core(self, p, s):
+        a = self.at
+        r = self.bufs[p].at[self.slot(s), :, a.cb]
+        return self.put(r, r, self.ps.at[p, s, 4], self.pr.at[p, s, 4], a.core)
+    def start_z(self, p):
+        for s in (1, 2, 3):
+            self.c_z(p, s).start()
+    def st1(self, p, s):
+        if s:
+            self.c_z(p, s).wait_recv()
+        for j in (0, 1):
+            self.c_xy(p, s, j).start()
+    def st2(self, p, s):
+        for j in (0, 1):
+            self.c_xy(p, s, j).wait_recv()
+            self.c_half(p, s, j).start()
+    def st3(self, p, s):
+        for j in (0, 1):
+            self.c_half(p, s, j).wait_recv()
+        self.c_core(p, s).start()
+    def st4(self, p, s):
+        self.c_core(p, s).wait_recv()
+    def drain(self, p):
+        for s in (1, 2, 3):
+            self.c_z(p, s).wait_send()
+        for s in range(4):
+            for j in (0, 1):
+                self.c_xy(p, s, j).wait_send()
+                self.c_half(p, s, j).wait_send()
+            self.c_core(p, s).wait_send()
+
+def gather_kernel(inner, w_ref, oa, ob, oc, od, ga, gb, gc, gd, zs, zr, ps, pr, ls):
+    at = Place(inner)
+    bufs = (ga, gb, gc, gd)
+    barrier([at.core, at.xn, at.yn] + [at.zdev(s) for s in (1, 2, 3)])
+    own = [w_ref.at[:, pl.ds(OFF[p], COLS[p])] for p in range(4)]
+    g = Gather(at, own, bufs, (zs, zr, ps, pr))
+    g.start_z(0)
+    for p in range(4):
+        bufs[p][at.z, at.yx, at.cb] = own[p][...]
+    seq = [(p, s) for p in range(4) for s in range(4)]
+    n = len(seq)
+    for i in range(-1, n + 3):
+        if i >= 0 and i % 4 == 0 and i // 4 + 1 < 4:
+            g.start_z(i // 4 + 1)
+        if i + 1 < n:
+            g.st1(*seq[i + 1])
+        if 0 <= i - 1 < n:
+            g.st2(*seq[i - 1])
+        if 0 <= i - 2 < n:
+            g.st3(*seq[i - 2])
+        if 0 <= i - 3 < n:
+            g.st4(*seq[i - 3])
+    for p in range(4):
+        g.drain(p)
+    copies = [pltpu.make_async_copy(b, o, ls.at[p]) for p, (b, o) in enumerate(zip(bufs, (oa, ob, oc, od)))]
+    for copy in copies:
+        copy.start()
+    for copy in copies:
+        copy.wait()
+
+
+def gathered(pack, inner):
+    dma = pltpu.SemaphoreType.DMA
+    return pl.pallas_call(
+        functools.partial(gather_kernel, inner),
+        out_shape=[jax.ShapeDtypeStruct((TP, 4, 2, 96, c), jnp.bfloat16) for c in COLS],
+        in_specs=[pl.BlockSpec(memory_space=pltpu.VMEM)],
+        out_specs=[pl.BlockSpec(memory_space=pl.ANY)] * 4,
+        scratch_shapes=[pltpu.VMEM((TP, 4, 2, 96, c), jnp.bfloat16) for c in COLS]
+        + [dma((4, 3)), dma((4, 3)), dma((4, 4, 5)), dma((4, 4, 5)), dma((4,))],
+        compiler_params=pltpu.CompilerParams(
+            collective_id=0, has_side_effects=True, vmem_limit_bytes=40 << 20
+        ),
+    )(pack)
+
+
 def per_device(
     tokens, w_qkv, w_score, w_out, w_fc, w_proj, ln1_gain, ln2_gain, selected, holder, cotangent
 ):
-    whole = (
-        lax.all_gather(w_qkv, "dp", axis=0, tiled=True),
-        lax.all_gather(w_score, "dp", axis=0, tiled=True),
-        lax.all_gather(w_out, "dp", axis=1, tiled=True),
-        lax.all_gather(w_fc, "dp", axis=0, tiled=True),
-        lax.all_gather(w_proj, "dp", axis=1, tiled=True),
-        lax.all_gather(ln1_gain, "dp", axis=0, tiled=True),
-        lax.all_gather(ln2_gain, "dp", axis=0, tiled=True),
-    )
-    whole_qkv, whole_score, whole_out, whole_fc, whole_proj, gain_one, gain_two = whole
+    inner = lax.axis_size("dp") // 8
+    gains = jnp.stack([ln1_gain, ln2_gain], axis=1)
+    pack = jnp.concatenate(
+        [w_qkv, w_score, gains, jnp.zeros((w_qkv.shape[0], 59), jnp.bfloat16), w_out.T, jnp.zeros((w_qkv.shape[0], 64), jnp.bfloat16), w_fc, w_proj.T],
+        axis=1,
+    )
+    if inner > 1:
+        groups = [[o * inner + i for i in range(inner)] for o in range(8)]
+        pack = lax.all_gather(pack, "dp", axis=0, tiled=True, axis_index_groups=groups)
+    here = [
+        lax.dynamic_index_in_dim(g, lax.axis_index("tp"), 0, False).reshape(768, -1)
+        for g in gathered(pack, inner)
+    ]
+    whole_qkv, whole_score = here[0][:, :576], here[0][:, 576:579]
+    gain_one, gain_two = here[0][:, 579], here[0][:, 580]
+    whole_out, whole_fc, whole_proj = here[1][:, :192].T, here[2], here[3].T
     parts = lax.axis_size("tp")
     local_rows = tokens.shape[0]
     rows = local_rows * parts

time: 1310 us -> 1380 us (1.053)
  Pallas kernels: 0 us -> 79.3 us
  blocking collectives: 69.3 us -> 25.1 us
  local copies, waits for them, and re-layouts: 293 us -> 315 us
  waiting for transfers between devices: 611 us -> 629 us
    pallas_call x0 -> x1, Pallas kernels: none -> 79.3 us  [gathered(): pl.pallas_call(functools.partial(gather_kernel, inner), out_shape=[jax.Sh...]
    all_gather x1, waiting for transfers between devices: 30.9 us -> 63.2 us  [per_device(): first_full = lax.all_gather(first_low, 'tp', axis=0, tiled=True)]
    all_gather x3 -> x0, blocking collectives: 28.7 us -> none  [the longest x1 10.6 us: per_device(): lax.all_gather(w_out, 'dp', axis=1, tiled=True)]
    all_gather x1, waiting for transfers between devices: 29.1 us -> 56.1 us  [per_device(): upstream_full = lax.all_gather(cotangent, 'tp', axis=0, tiled=True)]
    all_gather x2 -> x0, waiting for transfers between devices: 17.9 us -> none  [the longest x1 17.9 us: per_device(): lax.all_gather(w_fc, 'dp', axis=0, tiled=True)]
    unnamed x2 -> x1, blocking collectives: 29.2 us -> 13.7 us
    reduce_scatter x1, waiting for transfers between devices: 74.5 us -> 59.2 us  [per_device(): lax.psum_scatter(product(attended, whole_out).astype(jnp.bfloat16), 'tp',...]
  transfers between devices with their start and end apart: 21 -> 19, of which waited for: 12 -> 11; matrix products, arithmetic and copies ran while one was open for 27% -> 26% of each run, Pallas kernels for 0% -> 0%
where the time goes in v1:
time: 1380 us; the launch traced here: 1370 us
  waiting for transfers between devices  629 us (46%)
  local copies, waits for them, and re-layouts  315 us (23%)
  other arithmetic  198 us (14%)
  matrix products  108 us (8%)
  Pallas kernels  79.3 us (6%)
  blocking collectives  25.1 us (2%)
  between operations  15.6 us (1%)
    gather x5, local copies, waits for them, and re-layouts, pick(): jnp.take_along_axis(table.transpose(1, 0, 2), picked[:, :, None], axis=1)  125 us
    scatter-add x3, other arithmetic, place(): spread_out = jnp.zeros((heads * rows, width), jnp.float32).at[flat_index]...  114 us
    reduce_scatter x1, waiting for transfers between devices, per_device(): lax.psum_scatter(times_trans(grad_pre, whole_fc), 'tp', scatter_dimension...  101 us
    pallas_call x1, Pallas kernels, gathered(): pl.pallas_call(functools.partial(gather_kernel, inner), out_shape=[jax.Sh...  79.3 us
    all_gather x1, waiting for transfers between devices, per_device(): lax.all_gather(grad_resid.astype(jnp.bfloat16), 'tp', axis=0, tiled=True)  63.4 us
    all_gather x1, waiting for transfers between devices, per_device(): first_full = lax.all_gather(first_low, 'tp', axis=0, tiled=True)  63.2 us
    reduce_scatter x1, waiting for transfers between devices, per_device(): lax.psum_scatter(product(hidden, whole_proj).astype(jnp.bfloat16), 'tp',...  60.5 us
    all_gather x1, waiting for transfers between devices, per_device(): second_full = lax.all_gather(second_low, 'tp', axis=0, tiled=True)  59.8 us
  transfers between devices with their start and end apart: 19, of which 11 were waited for; matrix products, arithmetic and copies ran while one was open for 26% of the time, Pallas kernels for 0%

profile of v1, /device:TPU:0, one launch (start us, length us, event | category | flops | bytes accessed | tf_op | source)
XLA Modules:
  0.0 1371.8 jit_solution(13387030937950956321)
XLA Ops:
  14.7 79.3 %shard_map.178 = (bf16[4,4,2,96,640]{4,3,2,1,0:T(8,128)(2,1)S(1)}, bf16[4,4,2,96,256]{4,3,2,1,0:T(8,128)(2,1)S(1)}, bf16[4,4,2,96,768]{4,3,2,1,0:T(8,128)(2,1)S(1)}, bf16[4,4,2,96,768]{4,3,2,1,0:T(8,128)(2,1)}) custom-call(bf16[96,2432]{1,0:T(8,128)(2,1)S(1)} %concatenate.36.w_ref), custom_call_target="tpu_custom_call" | custom-call | tf_op jit(solution)/shard_map/pallas_call | solution.py:174
  104.1 63.2 %all-gather.5.cloned.1.call-done = bf16[2048,768]{1,0:T(8,128)(2,1)} async-done(((bf16[512,768]{1,0:T(8,128)(2,1)}), bf16[2048,768]{1,0:T(8,128)(2,1)}) %all-gather.5.cloned.1.call-update) | async-done | bytes 3145744 | tf_op jit(solution)/shard_map/all_gather | solution.py:219
  206.2 52.4 %gather_fusion = bf16[6144]{0:T(1024)(128)(2,1)S(1)} fusion(bf16[3,2048]{1,0:T(4,128)(2,1)S(1)} %bitcast.170, s32[6144]{0:T(1024)S(1)} %reshape.448), kind=kCustom, calls=%fused_computation.2 | custom fusion | bytes 73728 | tf_op jit(solution)/shard_map/jit(take_along_axis)/gather | solution.py:260
  260.7 60.6 %gather_fusion.2 = bf16[6144,64]{1,0:T(8,128)(2,1)} fusion(bf16[3,2048,64]{2,1,0:T(8,128)(2,1)S(1)} %bitcast.172, s32[6144]{0:T(1024)S(1)} %reshape.448), kind=kCustom, calls=%fused_computation.1.clone | custom fusion | bytes 1622016 | tf_op jit(solution)/shard_map/jit(take_along_axis)/gather | solution.py:254
  325.5 60.6 %gather_fusion.1 = bf16[6144,64]{1,0:T(8,128)(2,1)} fusion(bf16[3,2048,64]{2,1,0:T(8,128)(2,1)S(1)} %bitcast.171, s32[6144]{0:T(1024)S(1)} %reshape.448), kind=kCustom, calls=%fused_computation.clone | custom fusion | bytes 1622016 | tf_op jit(solution)/shard_map/jit(take_along_axis)/gather | solution.py:254
  403.1 17.5 %fusion.119 = (f32[32,3,64]{2,1,0:T(4,128)S(1)}, f32[32,3,64,192]{3,2,1,0:T(8,128)S(1)}) fusion(f32[32,3,64,64]{3,2,1,0:T(8,128)S(1)} %multiply_add_fusion, f32[32,3,64,128]{3,2,1,0:T(8,128)S(1)} %copy-done.31, pred[32,3,64,64]{3,2,1,0:T(8,128)(4,1)S(1)} %broadcast_in_dim.50, pred[32,3,64,128]{3,2,1,0:T(8,128)(4,1)S(1)} %broadcast_in_dim.49), kind=kOutput, calls=%fused_computation.239 | output fusion | flops 9437375 | bytes 10641408 | tf_op jit(solution)/shard_map/sub | solution.py:292
  438.4 59.2 %reduce-scatter.14.cloned.1.call-done = bf16[512,768]{1,0:T(8,128)(2,1)} async-done(((bf16[2048,768]{1,0:T(8,128)(2,1)}), bf16[512,768]{1,0:T(8,128)(2,1)}) %reduce-scatter.14.cloned.1.call-update) | async-done | bytes 786448 | tf_op jit(solution)/shard_map/reduce_scatter | solution.py:308
  505.8 59.8 %all-gather.7.cloned.1.call-done = bf16[2048,768]{1,0:T(8,128)(2,1)} async-done(((bf16[512,768]{1,0:T(8,128)(2,1)}), bf16[2048,768]{1,0:T(8,128)(2,1)}) %all-gather.7.cloned.1.call-update) | async-done | bytes 3145744 | tf_op jit(solution)/shard_map/all_gather | solution.py:314
  573.2 56.1 %all-gather.9.cloned.1.call-done = bf16[2048,768]{1,0:T(8,128)(2,1)} async-done(((bf16[512,768]{1,0:T(8,128)(2,1)}), bf16[2048,768]{1,0:T(8,128)(2,1)}) %all-gather.9.cloned.1.call-update) | async-done | bytes 3145744 | tf_op jit(solution)/shard_map/all_gather | solution.py:320
  643.9 8.7 convolution_convert_fusion
  652.7 100.8 %reduce-scatter.18.cloned.1.call-done = f32[512,768]{1,0:T(8,128)} async-done(((f32[2048,768]{1,0:T(8,128)}), f32[512,768]{1,0:T(8,128)}) %reduce-scatter.18.cloned.1.call-update) | async-done | bytes 1572880 | tf_op jit(solution)/shard_map/reduce_scatter | solution.py:325
  755.9 60.5 %reduce-scatter.16.cloned.1.call-done = bf16[512,768]{1,0:T(8,128)(2,1)} async-done(((bf16[2048,768]{1,0:T(8,128)(2,1)}), bf16[512,768]{1,0:T(8,128)(2,1)}) %reduce-scatter.16.cloned.1.call-update) | async-done | bytes 786448 | tf_op jit(solution)/shard_map/reduce_scatter | solution.py:317
  821.6 63.4 %all-gather.11.cloned.1.call-done = bf16[2048,768]{1,0:T(8,128)(2,1)} async-done(((bf16[512,768]{1,0:T(8,128)(2,1)}), bf16[2048,768]{1,0:T(8,128)(2,1)}) %all-gather.11.cloned.1.call-update) | async-done | bytes 3145744 | tf_op jit(solution)/shard_map/all_gather | solution.py:332
  898.0 36.7 %multiply_convert_fusion = bf16[32,3,64,192]{3,2,1,0:T(8,128)(2,1)S(1)} fusion(f32[32,3,64,64]{3,2,1,0:T(8,128)S(1)} %fusion.51, f32[32,3,64,128]{3,2,1,0:T(8,128)S(1)} %fusion.53, f32[32,3,64,192]{3,2,1,0:T(8,128)} %copy-done.21, f32[32,3,64]{2,1,0:T(4,128)S(1)} %get-tuple-element.44), kind=kOutput, calls=%fused_computation.25 | output fusion | flops 9443519 | bytes 11821056 | tf_op jit(solution)/shard_map/sub | solution.py:345
  946.9 43.1 %scatter_custom_fusion.2 = f32[6144]{0:T(1024)S(1)} fusion(s32[6144]{0:T(1024)S(1)} %bitcast.199, f32[6144]{0:T(1024)S(1)} %reshape.440, f32[]{:T(128)} %constant.176.clone.1), kind=kCustom, calls=%fused_computation.184 | custom fusion | flops 6144 | bytes 24580 | tf_op jit(solution)/shard_map/scatter-add | solution.py:387
  990.1 35.4 %scatter_custom_fusion = f32[6144,64]{1,0:T(8,128)} fusion(s32[6144]{0:T(1024)S(1)} %bitcast.200, f32[6144,64]{1,0:T(8,128)} %bitcast.184, f32[]{:T(128)} %constant.176.clone.1), kind=kCustom, calls=%fused_computation.79 | custom fusion | flops 393216 | bytes 1573376 | tf_op jit(solution)/shard_map/scatter-add | solution.py:387
  1035.2 35.3 %scatter_custom_fusion.1 = f32[6144,64]{1,0:T(8,128)} fusion(s32[6144]{0:T(1024)S(1)} %bitcast.201, f32[6144,64]{1,0:T(8,128)} %bitcast.185, f32[]{:T(128)} %constant.176.clone.1), kind=kCustom, calls=%fused_computation.77 | custom fusion | flops 393216 | bytes 1573376 | tf_op jit(solution)/shard_map/scatter-add | solution.py:387
  1149.9 8.4 fusion.116
  1169.5 58.0 %reduce-scatter.20.cloned.1.call-done = bf16[512,768]{1,0:T(8,128)(2,1)} async-done(((bf16[2048,768]{1,0:T(8,128)(2,1)}), bf16[512,768]{1,0:T(8,128)(2,1)}) %reduce-scatter.20.cloned.1.call-update) | async-done | bytes 786448 | tf_op jit(solution)/shard_map/reduce_scatter | solution.py:407
  1229.6 13.7 all-reduce.7
  1243.5 11.4 all-reduce.8
  1257.7 16.4 %reduce-scatter.24.cloned.1.call-done = f32[96,768]{1,0:T(8,128)} async-done(((f32[768,768]{1,0:T(8,128)}), f32[96,768]{1,0:T(8,128)}) %reduce-scatter.24.cloned.1.call-update) | async-done | bytes 294928 | tf_op jit(solution)/shard_map/reduce_scatter | solution.py:424
  1274.1 46.6 %reduce-scatter.26.cloned.1.call-done = f32[768,96]{0,1:T(8,128)} async-done(((f32[768,768]{0,1:T(8,128)}), f32[768,96]{0,1:T(8,128)}) %reduce-scatter.26.cloned.1.call-update) | async-done | bytes 294928 | tf_op jit(solution)/shard_map/reduce_scatter | solution.py:425
  1320.7 44.3 %reduce-scatter.22.cloned.1.call-done = f32[96,576]{1,0:T(8,128)} async-done(((f32[768,576]{1,0:T(8,128)}), f32[96,576]{1,0:T(8,128)}) %reduce-scatter.22.cloned.1.call-update) | async-done | bytes 221200 | tf_op jit(solution)/shard_map/reduce_scatter | solution.py:421
  (275 shorter events, 264.8 us)
Async XLA Ops:
  7.2 93.4 %copy-start.2 = (bf16[512,768]{1,0:T(8,128)(2,1)S(1)}, bf16[512,768]{1,0:T(8,128)(2,1)}, u32[]{:S(2)}) copy-start(bf16[512,768]{1,0:T(8,128)(2,1)} %param.13) | copy-start | bytes 2359300
  7.2 160.1 %all-gather.5.cloned.1.call-start = ((), (), s32[]{:S(2)}) async-start(), calls=%async_computation.9 | async-start | bytes 3932160 | tf_op jit(solution)/shard_map/all_gather | solution.py:219
  8.6 93.1 %copy-start.38 = (f32[512]{0:T(512)}, f32[512]{0:T(512)S(1)}, u32[]{:S(2)}) copy-start(f32[512]{0:T(512)S(1)} %broadcast_multiply_fusion.5) | copy-start | bytes 6148
  10.1 91.6 %copy-start.40 = (f32[512]{0:T(512)}, f32[512]{0:T(512)S(1)}, u32[]{:S(2)}) copy-start(f32[512]{0:T(512)S(1)} %add_rsqrt_fusion.1) | copy-start | bytes 6148
  13.4 88.9 %copy-start.35 = (s32[32,3,64]{2,0,1:T(8,128)S(1)}, s32[32,3,64]{2,0,1:T(8,128)}, u32[]{:S(2)}) copy-start(s32[32,3,64]{2,0,1:T(8,128)} %param.21) | copy-start | bytes 73732
  101.8 395.8 %reduce-scatter.14.cloned.1.call-start = ((), (), s32[]{:S(2)}) async-start(), calls=%async_computation.10 | async-start | bytes 3932160 | tf_op jit(solution)/shard_map/reduce_scatter | solution.py:308
  174.7 84.2 %collective-permute-start.2 = (bf16[2048,3,64]{0,2,1:T(8,128)(2,1)}, bf16[2048,3,64]{0,2,1:T(8,128)(2,1)}, u32[]{:S(2)}, u32[]{:S(2)}) collective-permute-start(bf16[2048,3,64]{0,2,1:T(8,128)(2,1)} %get-tuple-element.32), channel_id=1, source_target_pairs={{0,4},{4,0},{8,12},{12,8},{16,20},{20,16},{24,28},{28,24},{1,5},{5... | collective-permute-start | bytes 2359304 | tf_op jit(solution)/shard_map/ppermute | solution.py:24
  174.7 149.1 %collective-permute-start = (bf16[2048,3,64]{0,2,1:T(8,128)(2,1)}, bf16[2048,3,64]{0,2,1:T(8,128)(2,1)}, u32[]{:S(2)}, u32[]{:S(2)}) collective-permute-start(bf16[2048,3,64]{0,2,1:T(8,128)(2,1)} %get-tuple-element.33), channel_id=1, source_target_pairs={{0,4},{4,0},{8,12},{12,8},{16,20},{20,16},{24,28},{28,24},{1,5},{5... | collective-permute-start | bytes 2359304 | tf_op jit(solution)/shard_map/ppermute | solution.py:24
  177.7 28.5 %collective-permute-start.1 = (bf16[2048,3]{0,1:T(4,128)(2,1)S(1)}, bf16[2048,3]{0,1:T(4,128)(2,1)S(1)}, u32[]{:S(2)}, u32[]{:S(2)}) collective-permute-start(bf16[2048,3]{0,1:T(4,128)(2,1)S(1)} %get-tuple-element.42), channel_id=1, source_target_pairs={{0,4},{4,0},{8,12},{12,8},{16,20},{20,16},{24,28},{28,24},{1,5},{5... | collective-permute-start | bytes 36872 | tf_op jit(solution)/shard_map/ppermute | solution.py:24
  438.4 127.3 %all-gather.7.cloned.1.call-start = ((), (), s32[]{:S(2)}) async-start(), calls=%async_computation.11 | async-start | bytes 3932160 | tf_op jit(solution)/shard_map/all_gather | solution.py:314
  502.0 127.3 %all-gather.9.cloned.1.call-start = ((), (), s32[]{:S(2)}) async-start(), calls=%async_computation.13 | async-start | bytes 3932160 | tf_op jit(solution)/shard_map/all_gather | solution.py:320
  502.6 250.9 %reduce-scatter.18.cloned.1.call-start = ((), (), s32[]{:S(2)}) async-start(), calls=%async_computation.14 | async-start | bytes 7864320 | tf_op jit(solution)/shard_map/reduce_scatter | solution.py:325
  643.9 172.5 %reduce-scatter.16.cloned.1.call-start = ((), (), s32[]{:S(2)}) async-start(), calls=%async_computation.12 | async-start | bytes 3932160 | tf_op jit(solution)/shard_map/reduce_scatter | solution.py:317
  652.6 232.3 %all-gather.11.cloned.1.call-start = ((), (), s32[]{:S(2)}) async-start(), calls=%async_computation.15 | async-start | bytes 3932160 | tf_op jit(solution)/shard_map/all_gather | solution.py:332
  821.3 345.2 %reduce-scatter.28.cloned.1.call-start = ((), (), s32[]{:S(2)}) async-start(), calls=%async_computation.20 | async-start | bytes 442368
  990.0 83.6 %collective-permute-start.5 = (bf16[2048,3]{0,1:T(4,128)(2,1)S(1)}, bf16[2048,3]{0,1:T(4,128)(2,1)S(1)}, u32[]{:S(2)}, u32[]{:S(2)}) collective-permute-start(bf16[2048,3]{0,1:T(4,128)(2,1)S(1)} %bitcast.202), channel_id=1, source_target_pairs={{0,4},{4,0},{8,12},{12,8},{16,20},{20,16},{24,28},{28,24},{1,5},{5... | collective-permute-start | bytes 36872 | tf_op jit(solution)/shard_map/ppermute | solution.py:24
  1030.6 101.1 %collective-permute-start.3 = (bf16[2048,3,64]{0,2,1:T(8,128)(2,1)}, bf16[2048,3,64]{0,2,1:T(8,128)(2,1)}, u32[]{:S(2)}, u32[]{:S(2)}) collective-permute-start(bf16[2048,3,64]{0,2,1:T(8,128)(2,1)} %bitcast.169), channel_id=1, source_target_pairs={{0,4},{4,0},{8,12},{12,8},{16,20},{20,16},{24,28},{28,24},{1,5},{5... | collective-permute-start | bytes 2359304 | tf_op jit(solution)/shard_map/ppermute | solution.py:24
  1073.5 60.3 %collective-permute-start.4 = (bf16[2048,3,64]{0,2,1:T(8,128)(2,1)}, bf16[2048,3,64]{0,2,1:T(8,128)(2,1)}, u32[]{:S(2)}, u32[]{:S(2)}) collective-permute-start(bf16[2048,3,64]{0,2,1:T(8,128)(2,1)} %bitcast.167), channel_id=1, source_target_pairs={{0,4},{4,0},{8,12},{12,8},{16,20},{20,16},{24,28},{28,24},{1,5},{5... | collective-permute-start | bytes 2359304 | tf_op jit(solution)/shard_map/ppermute | solution.py:24
  1077.2 90.7 %reduce-scatter.30.cloned.1.call-start = ((), (), s32[]{:S(2)}) async-start(), calls=%async_computation.21 | async-start | bytes 884736
  1131.2 96.3 %reduce-scatter.20.cloned.1.call-start = ((), (), s32[]{:S(2)}) async-start(), calls=%async_computation.16 | async-start | bytes 3932160 | tf_op jit(solution)/shard_map/reduce_scatter | solution.py:407
  1142.8 131.2 %reduce-scatter.24.cloned.1.call-start = ((), (), s32[]{:S(2)}) async-start(), calls=%async_computation.18 | async-start | bytes 2654208 | tf_op jit(solution)/shard_map/reduce_scatter | solution.py:424
  1149.8 170.9 %reduce-scatter.26.cloned.1.call-start = ((), (), s32[]{:S(2)}) async-start(), calls=%async_computation.19 | async-start | bytes 2654208 | tf_op jit(solution)/shard_map/reduce_scatter | solution.py:425
  1158.3 206.8 %reduce-scatter.22.cloned.1.call-start = ((), (), s32[]{:S(2)}) async-start(), calls=%async_computation.17 | async-start | bytes 2211840 | tf_op jit(solution)/shard_map/reduce_scatter | solution.py:421
  1165.1 89.7 %copy-start.22 = (f32[512,768]{1,0:T(8,128)S(1)}, f32[512,768]{1,0:T(8,128)}, u32[]{:S(2)}) copy-start(f32[512,768]{1,0:T(8,128)} %get-tuple-element.31) | copy-start | bytes 4718596
  (40 other events, 484.8 us)
Sparse Core Ops, SparseCore 0:
  101.9 65.3 all-gather.4
  438.5 59.0 reduce-scatter.13
  502.1 63.5 all-gather.6
  567.1 62.1 all-gather.8
  644.0 109.3 reduce-scatter.17
  755.6 60.7 reduce-scatter.15
  821.4 63.5 all-gather.10
  1077.4 32.6 reduce-scatter.27
  1131.4 33.7 reduce-scatter.29
  1167.3 60.2 reduce-scatter.19
  1231.5 42.5 reduce-scatter.23
  1278.2 42.4 reduce-scatter.25
  1324.7 40.2 reduce-scatter.21
